TPU v7x, 32 devices: a whole 2x2x4 slice. The times are simulated.
32 devices in a mesh: blk: 4 (over y, core), reader: 2 (over x), bulk: 4 (over z).
Axes of the slice: x: 2, y: 2, z: 4, core: 2. Of those that a mesh axis runs over, the one named last changes fastest.
Arguments:
- vectors: float32 [128, 8192], P('bulk', ('blk', 'reader')), may hold values from -6 to 6
- ham_tiles: float32 [8, 4, 24, 128, 128], P(('blk', 'reader'))
- tile_rows: int32 [8, 4, 24], P(('blk', 'reader')), may hold values from 0 to 7, as said below
- tile_cols: int32 [8, 4, 24], P(('blk', 'reader')), may hold values from 0 to 15
- center: float32 [1], replicated, may hold values from -0.5 to 0.5
- halfwidth: float32 [1], replicated, may hold values from 1 to 2
Outputs:
- filtered: float32 [128, 8192], P('bulk', ('blk', 'reader'))
Inputs may be any that keep to these rules, and one draw needn't show every extreme that they name: tile_rows and tile_cols of one panel together name 24 different tiles.
All inputs are finite; a program needn't handle non-finite values.
Results may differ from a plain program's by a relative error of at most 0.0003.
Values sent between devices are 32-bit elements; how exact they have to be, the bound alone decides.
A program may use at most 64 MiB of HBM per device.

v0:
```python
import functools

import jax
import jax.numpy as jnp
from jax import lax
from jax.experimental import pallas as pl
from jax.experimental.pallas import tpu as pltpu
from jax.sharding import PartitionSpec as P

TILE = 128
PASSES = 2
DEGREE = 3
CORES = 2


def kernel(
    n_blk, n_reader, total_cols,
    vec_ref, ham_ref, rows_ref, cols_ref, center_ref, half_ref,
    out_ref,
    blocks, sources, staged, weights, acc, before, scale, sums, partial_sum,
    ham_sem,
    send_x, send_y, send_dx, send_dy, send_own, send_cx, send_cy, send_cdx, send_cdy,
    recv_x, recv_y, recv_dx, recv_dy, recv_own, recv_cx, recv_cy, recv_cdx, recv_cdy,
    send_sum, recv_sum,
):
    vecs = vec_ref.shape[0]
    row_tiles = vec_ref.shape[1] // TILE
    slots = rows_ref.shape[2]
    group_tiles = n_reader * row_tiles
    peers = n_blk * n_reader - 1
    half = vecs // 2
    halves = (pl.ds(0, half), pl.ds(half, half))

    blk = lax.axis_index("blk")
    x = lax.axis_index("reader")
    core = lax.rem(blk, CORES)
    side = blk - core
    blk_c = side + (1 - core)
    blk_y = lax.rem(blk + CORES, n_blk)
    blk_yc = lax.rem(blk_c + CORES, n_blk)
    me = blk * n_reader + x

    def peer(step):
        other = lax.rem(me + step, n_blk * n_reader)
        return {"blk": other // n_reader, "reader": lax.rem(other, n_reader)}

    def block_of(b, step=0):
        return b * n_reader + lax.rem(x + n_reader - step, n_reader)

    barrier = pltpu.get_barrier_semaphore()
    for step in range(1, peers + 1):
        pl.semaphore_signal(
            barrier, inc=1, device_id=peer(step), device_id_type=pl.DeviceIdType.MESH
        )

    def ham_copy(group):
        return pltpu.make_async_copy(
            ham_ref.at[0, group], staged.at[group], ham_sem.at[group]
        )

    for group in (blk, blk_c, blk_y, blk_yc):
        ham_copy(group).start()
    blocks[0, me] = vec_ref[...]
    scale[...] = jnp.ones_like(scale)
    before[...] = jnp.zeros_like(before)
    pl.semaphore_wait(barrier, peers)

    def split_tiles(group):
        ham_copy(group).wait()

        def one(slot, carry):
            tile = staged[group, slot]
            high = tile.astype(jnp.bfloat16)
            low = (tile - high.astype(jnp.float32)).astype(jnp.bfloat16)
            weights[group * slots + slot] = jnp.concatenate([high, low], axis=1)
            return carry

        lax.fori_loop(0, slots, one, 0)

    def split_block(par, index):
        for t in range(row_tiles):
            value = blocks[par, index, :, t * TILE : (t + 1) * TILE] * scale[...]
            high = value.astype(jnp.bfloat16)
            low = (value - high.astype(jnp.float32)).astype(jnp.bfloat16)
            sources[index * row_tiles + t] = jnp.concatenate([high, low], axis=0)

    unroll = max(u for u in (8, 6, 4, 3, 2, 1) if slots % u == 0)

    def multiply(group):
        def some(turn, carry):
            carry = list(carry)
            for u in range(unroll):
                slot = turn * unroll + u
                col = cols_ref[0, group, slot]
                row = rows_ref[0, group, slot]
                source = sources[group * group_tiles + col]
                product = lax.dot_general(
                    jnp.concatenate([source, source], axis=1),
                    weights[group * slots + slot],
                    (((1,), (1,)), ((), ())),
                    preferred_element_type=jnp.float32,
                )
                product = product[:vecs] + product[vecs:]
                for t in range(row_tiles):
                    carry[t] = carry[t] + jnp.where(row == t, product, 0.0)
            return tuple(carry)

        start = tuple(acc[t] for t in range(row_tiles))
        done = lax.fori_loop(0, slots // unroll, some, start)
        for t in range(row_tiles):
            acc[t] = done[t]

    def remote(par, index, part, send, recv, target):
        where = blocks.at[par, index] if part is None else blocks.at[par, index, halves[part]]
        return pltpu.make_async_remote_copy(
            src_ref=where, dst_ref=where, send_sem=send, recv_sem=recv,
            device_id=target, device_id_type=pl.DeviceIdType.MESH,
        )

    to_core = {"blk": blk_c}
    to_y = {"blk": blk_y}

    def to_x(step):
        return {"reader": lax.rem(x + step, n_reader)}

    steps = range(1, n_reader)

    def sum_copy(turn, step):
        return pltpu.make_async_remote_copy(
            src_ref=partial_sum.at[turn], dst_ref=sums.at[turn, step - 1],
            send_sem=send_sum.at[turn, step - 1], recv_sem=recv_sum.at[turn, step - 1],
            device_id=peer(step), device_id_type=pl.DeviceIdType.MESH,
        )

    diagonal = (
        lax.broadcasted_iota(jnp.int32, (vecs, TILE), 0)
        == lax.broadcasted_iota(jnp.int32, (vecs, TILE), 1)
    )

    def share_sums(turn, squares):
        own = jnp.sum(squares, axis=1, keepdims=True)
        line = jnp.sum(jnp.where(diagonal, own, 0.0), axis=0, keepdims=True)
        partial_sum[turn] = jnp.broadcast_to(line, partial_sum.shape[1:])
        for step in range(1, peers + 1):
            sum_copy(turn, step).start()

    def norms(turn):
        for step in range(1, peers + 1):
            sum_copy(turn, step).wait()
        total = partial_sum[turn]
        for step in range(1, peers + 1):
            total = total + sums[turn, step - 1]
        spread = jnp.broadcast_to(total[:1], (vecs, TILE))
        squares = jnp.sum(jnp.where(diagonal, spread, 0.0), axis=1, keepdims=True)
        root = jnp.sqrt(squares / total_cols + 1e-06)
        return jnp.broadcast_to(1.0 / root, (vecs, TILE))

    def apply(k, carry):
        par = lax.rem(k, 2)
        x_own = [[remote(par, me, h, send_x.at[s - 1, h], recv_x.at[par, s - 1, h], to_x(s))
                  for h in range(2)] for s in steps]
        y_own = [remote(par, me, h, send_y.at[h], recv_y.at[par, h], to_y) for h in range(2)]
        c_own = remote(par, me, None, send_own, recv_own.at[par], to_core)
        x_block = [block_of(blk, s) for s in steps]
        y_block = block_of(blk_y)
        d_block = [block_of(blk_y, s) for s in steps]
        dy = [remote(par, x_block[s - 1], 0, send_dy.at[s - 1], recv_dy.at[par, s - 1], to_y)
              for s in steps]
        dx = [remote(par, y_block, 1, send_dx.at[s - 1], recv_dx.at[par, s - 1], to_x(s))
              for s in steps]
        cx = [[remote(par, x_block[s - 1], h, send_cx.at[s - 1, h],
                      recv_cx.at[par, s - 1, h], to_core) for h in range(2)] for s in steps]
        cy = [remote(par, y_block, h, send_cy.at[h], recv_cy.at[par, h], to_core)
              for h in range(2)]
        cdy = [remote(par, d_block[s - 1], 0, send_cdy.at[s - 1], recv_cdy.at[par, s - 1],
                      to_core) for s in steps]
        cdx = [remote(par, d_block[s - 1], 1, send_cdx.at[s - 1], recv_cdx.at[par, s - 1],
                      to_core) for s in steps]

        for s in steps:
            x_own[s - 1][0].start()
        y_own[1].start()
        c_own.start()
        for s in steps:
            x_own[s - 1][1].start()
        y_own[0].start()

        acc[...] = jnp.zeros_like(acc)

        @pl.when(k == 0)
        def _():
            split_tiles(blk)
            split_tiles(blk_c)

        @pl.when(k == DEGREE)
        def _():
            scale[...] = norms(0)

        @pl.when(k == DEGREE + 1)
        def _():
            scale[...] = jnp.ones_like(scale)

        split_block(par, me)
        for s in steps:
            x_own[s - 1][0].wait_recv()
            dy[s - 1].start()
            cx[s - 1][0].start()
        y_own[1].wait_recv()
        for s in steps:
            dx[s - 1].start()
        cy[1].start()
        for s in steps:
            x_own[s - 1][1].wait_recv()
            cx[s - 1][1].start()
            split_block(par, x_block[s - 1])
        y_own[0].wait_recv()
        cy[0].start()
        split_block(par, y_block)
        c_own.wait_recv()
        split_block(par, block_of(blk_c))
        multiply(blk)

        @pl.when(k == 0)
        def _():
            split_tiles(blk_y)
            split_tiles(blk_yc)

        for s in steps:
            dy[s - 1].wait_recv()
            cdy[s - 1].start()
            dx[s - 1].wait_recv()
            cdx[s - 1].start()
            split_block(par, d_block[s - 1])
        for s in steps:
            cx[s - 1][0].wait_recv()
            cx[s - 1][1].wait_recv()
            split_block(par, block_of(blk_c, s))
        multiply(blk_c)
        multiply(blk_y)
        cy[1].wait_recv()
        cy[0].wait_recv()
        split_block(par, block_of(blk_yc))
        for s in steps:
            cdy[s - 1].wait_recv()
            cdx[s - 1].wait_recv()
            split_block(par, block_of(blk_yc, s))
        multiply(blk_yc)

        first = lax.rem(k, DEGREE) == 0
        center = center_ref[0]
        gain = jnp.where(first, 1.0, 2.0) / half_ref[0]
        squares = jnp.zeros((vecs, TILE), jnp.float32)
        for t in range(row_tiles):
            lanes = slice(t * TILE, (t + 1) * TILE)
            field = blocks[par, me, :, lanes] * scale[...]
            new = (acc[t] - center * field) * gain
            new = new - jnp.where(first, 0.0, before[:, lanes])
            before[:, lanes] = field
            blocks[1 - par, me, :, lanes] = new
            squares = squares + new * new

        @pl.when(lax.rem(k, DEGREE) == DEGREE - 1)
        def _():
            share_sums(k // DEGREE, squares)

        c_own.wait_send()
        for h in range(2):
            y_own[h].wait_send()
            cy[h].wait_send()
        for s in steps:
            for h in range(2):
                x_own[s - 1][h].wait_send()
                cx[s - 1][h].wait_send()
            for copy in (dx, dy, cdx, cdy):
                copy[s - 1].wait_send()
        return carry

    lax.fori_loop(0, PASSES * DEGREE, apply, 0)
    last = norms(PASSES - 1)
    for t in range(row_tiles):
        lanes = slice(t * TILE, (t + 1) * TILE)
        out_ref[:, lanes] = blocks[PASSES * DEGREE % 2, me, :, lanes] * last


def shards(n_blk, n_reader, vectors, ham_tiles, tile_rows, tile_cols, center, halfwidth):
    vecs, width = vectors.shape
    row_tiles = width // TILE
    n = n_blk * n_reader
    groups, slots = tile_rows.shape[1:]
    others = n_reader - 1
    dma = pltpu.SemaphoreType.DMA
    smem = pl.BlockSpec(memory_space=pltpu.SMEM)
    vmem = pl.BlockSpec(memory_space=pltpu.VMEM)
    body = functools.partial(kernel, n_blk, n_reader, n * width)
    return pl.pallas_call(
        body,
        out_shape=jax.ShapeDtypeStruct((vecs, width), jnp.float32),
        in_specs=[vmem, pl.BlockSpec(memory_space=pl.ANY), smem, smem, smem, smem],
        out_specs=vmem,
        scratch_shapes=[
            pltpu.VMEM((2, n, vecs, width), jnp.float32),
            pltpu.VMEM((n * row_tiles, 2 * vecs, TILE), jnp.bfloat16),
            pltpu.VMEM((groups, slots, TILE, TILE), jnp.float32),
            pltpu.VMEM((groups * slots, TILE, 2 * TILE), jnp.bfloat16),
            pltpu.VMEM((row_tiles, vecs, TILE), jnp.float32),
            pltpu.VMEM((vecs, width), jnp.float32),
            pltpu.VMEM((vecs, TILE), jnp.float32),
            pltpu.VMEM((PASSES, n - 1, 8, TILE), jnp.float32),
            pltpu.VMEM((PASSES, 8, TILE), jnp.float32),
            dma((groups,)),
            dma((others, 2)), dma((2,)), dma((others,)), dma((others,)), dma,
            dma((others, 2)), dma((2,)), dma((others,)), dma((others,)),
            dma((2, others, 2)), dma((2, 2)), dma((2, others)), dma((2, others)), dma((2,)),
            dma((2, others, 2)), dma((2, 2)), dma((2, others)), dma((2, others)),
            dma((PASSES, n - 1)), dma((PASSES, n - 1)),
        ],
        compiler_params=pltpu.CompilerParams(
            collective_id=0, has_side_effects=True, vmem_limit_bytes=48 * 2**20
        ),
        cost_estimate=pl.CostEstimate(
            flops=PASSES * DEGREE * groups * slots * 8 * vecs * TILE * TILE,
            bytes_accessed=groups * slots * TILE * TILE * 4,
            transcendentals=0,
        ),
    )(vectors, ham_tiles, tile_rows, tile_cols, center, halfwidth)


def solution(mesh):
    n_blk, n_reader = mesh.shape["blk"], mesh.shape["reader"]
    return jax.shard_map(
        functools.partial(shards, n_blk, n_reader),
        mesh=mesh,
        in_specs=(
            P("bulk", ("blk", "reader")),
            P(("blk", "reader"), None, None, None, None),
            P(("blk", "reader"), None, None),
            P(("blk", "reader"), None, None),
            P(),
            P(),
        ),
        out_specs=P("bulk", ("blk", "reader")),
        check_vma=False,
    )
```

profile of v0, /device:TPU:0, one launch (start us, length us, event | category | flops | bytes accessed | tf_op | source)
XLA Modules:
  0.0 71.8 jit_solution(13422493448853811580)
XLA Ops:
  1.3 0.0 copy-start
  1.3 0.9 %copy-done = f32[32,1024]{1,0:T(8,128)S(1)} copy-done((f32[32,1024]{1,0:T(8,128)S(1)}, f32[32,1024]{1,0:T(8,128)}, u32[]{:S(2)}) %copy-start) | copy-done | bytes 131096
  2.2 0.0 copy-start.1
  2.2 0.7 copy-done.1
  2.9 0.0 copy-start.2
  2.9 0.7 copy-done.2
  3.6 67.6 %shard_map.64 = f32[32,1024]{1,0:T(8,128)S(1)} custom-call(f32[32,1024]{1,0:T(8,128)S(1)} %copy-done, f32[1,4,24,128,128]{4,3,2,1,0:T(8,128)} %ham_ref.1, s32[1,4,24]{2,1,0:T(4,128)S(1)} %copy-done.1, s32[1,4,24]{2,1,0:T(4,128)S(1)} %copy-done.2, f32[1]{0:T(128)S(6)} %copy.8.center_ref, f32[1]{0:T(128)S(6)} %copy.9.half_ref), custom_call_target="tpu_custom_call" | custom-call | flops 2415919104 | bytes 6291456 | tf_op jit(solution)/shard_map/pallas_call | solution.py:295
  71.2 0.7 copy.10
Async XLA Ops:
  1.3 0.9 %copy-start = (f32[32,1024]{1,0:T(8,128)S(1)}, f32[32,1024]{1,0:T(8,128)}, u32[]{:S(2)}) copy-start(f32[32,1024]{1,0:T(8,128)} %vec_ref.1) | copy-start | bytes 393220
  2.2 0.7 copy-start.1
  2.9 0.7 copy-start.2
where the time goes:
time: 72 us; the launch traced here: 71.8 us
  Pallas kernels  67.6 us (94%)
  local copies, waits for them, and re-layouts  2.92 us (4%)
  between operations  1.32 us (2%)
    pallas_call x1, Pallas kernels, shards(): pl.pallas_call(body, out_shape=jax.ShapeDtypeStruct((vecs, width), jnp.fl...  67.6 us
    unnamed x7, local copies, waits for them, and re-layouts  2.92 us

commit v1 on v0

--- a/solution.py
+++ b/solution.py
@@ -18,7 +18,7 @@
     vec_ref, ham_ref, rows_ref, cols_ref, center_ref, half_ref,
     out_ref,
     blocks, sources, staged, weights, acc, before, scale, sums, partial_sum,
-    ham_sem,
+    rows_smem, cols_smem, ham_sem, in_sem,
     send_x, send_y, send_dx, send_dy, send_own, send_cx, send_cy, send_cdx, send_cdy,
     recv_x, recv_y, recv_dx, recv_dy, recv_own, recv_cx, recv_cy, recv_cdx, recv_cdy,
     send_sum, recv_sum,
@@ -58,21 +58,29 @@
             ham_ref.at[0, group], staged.at[group], ham_sem.at[group]
         )
 
+    loads = [
+        pltpu.make_async_copy(vec_ref, blocks.at[0, me], in_sem.at[0]),
+        pltpu.make_async_copy(rows_ref.at[0], rows_smem, in_sem.at[1]),
+        pltpu.make_async_copy(cols_ref.at[0], cols_smem, in_sem.at[2]),
+    ]
+    for copy in loads:
+        copy.start()
     for group in (blk, blk_c, blk_y, blk_yc):
         ham_copy(group).start()
-    blocks[0, me] = vec_ref[...]
     scale[...] = jnp.ones_like(scale)
     before[...] = jnp.zeros_like(before)
+    for copy in loads:
+        copy.wait()
     pl.semaphore_wait(barrier, peers)
 
     def split_tiles(group):
         ham_copy(group).wait()
 
         def one(slot, carry):
-            tile = staged[group, slot]
+            tile = staged[group, slot].T
             high = tile.astype(jnp.bfloat16)
             low = (tile - high.astype(jnp.float32)).astype(jnp.bfloat16)
-            weights[group * slots + slot] = jnp.concatenate([high, low], axis=1)
+            weights[group * slots + slot] = jnp.concatenate([high, low], axis=0)
             return carry
 
         lax.fori_loop(0, slots, one, 0)
@@ -84,31 +92,22 @@
             low = (value - high.astype(jnp.float32)).astype(jnp.bfloat16)
             sources[index * row_tiles + t] = jnp.concatenate([high, low], axis=0)
 
-    unroll = max(u for u in (8, 6, 4, 3, 2, 1) if slots % u == 0)
-
     def multiply(group):
-        def some(turn, carry):
-            carry = list(carry)
-            for u in range(unroll):
-                slot = turn * unroll + u
-                col = cols_ref[0, group, slot]
-                row = rows_ref[0, group, slot]
-                source = sources[group * group_tiles + col]
-                product = lax.dot_general(
-                    jnp.concatenate([source, source], axis=1),
-                    weights[group * slots + slot],
-                    (((1,), (1,)), ((), ())),
-                    preferred_element_type=jnp.float32,
-                )
-                product = product[:vecs] + product[vecs:]
-                for t in range(row_tiles):
-                    carry[t] = carry[t] + jnp.where(row == t, product, 0.0)
-            return tuple(carry)
-
-        start = tuple(acc[t] for t in range(row_tiles))
-        done = lax.fori_loop(0, slots // unroll, some, start)
+        totals = [acc[t] for t in range(row_tiles)]
+        for slot in range(slots):
+            col = cols_smem[group, slot]
+            row = rows_smem[group, slot]
+            source = sources[group * group_tiles + col]
+            product = jnp.dot(
+                jnp.concatenate([source, source], axis=1),
+                weights[group * slots + slot],
+                preferred_element_type=jnp.float32,
+            )
+            product = product[:vecs] + product[vecs:]
+            for t in range(row_tiles):
+                totals[t] = totals[t] + jnp.where(row == t, product, 0.0)
         for t in range(row_tiles):
-            acc[t] = done[t]
+            acc[t] = totals[t]
 
     def remote(par, index, part, send, recv, target):
         where = blocks.at[par, index] if part is None else blocks.at[par, index, halves[part]]
@@ -219,6 +218,11 @@
         c_own.wait_recv()
         split_block(par, block_of(blk_c))
         multiply(blk)
+        for s in steps:
+            cx[s - 1][0].wait_recv()
+            cx[s - 1][1].wait_recv()
+            split_block(par, block_of(blk_c, s))
+        multiply(blk_c)
 
         @pl.when(k == 0)
         def _():
@@ -231,11 +235,6 @@
             dx[s - 1].wait_recv()
             cdx[s - 1].start()
             split_block(par, d_block[s - 1])
-        for s in steps:
-            cx[s - 1][0].wait_recv()
-            cx[s - 1][1].wait_recv()
-            split_block(par, block_of(blk_c, s))
-        multiply(blk_c)
         multiply(blk_y)
         cy[1].wait_recv()
         cy[0].wait_recv()
@@ -290,24 +289,27 @@
     others = n_reader - 1
     dma = pltpu.SemaphoreType.DMA
     smem = pl.BlockSpec(memory_space=pltpu.SMEM)
+    hbm = pl.BlockSpec(memory_space=pl.ANY)
     vmem = pl.BlockSpec(memory_space=pltpu.VMEM)
     body = functools.partial(kernel, n_blk, n_reader, n * width)
     return pl.pallas_call(
         body,
         out_shape=jax.ShapeDtypeStruct((vecs, width), jnp.float32),
-        in_specs=[vmem, pl.BlockSpec(memory_space=pl.ANY), smem, smem, smem, smem],
+        in_specs=[hbm, hbm, hbm, hbm, smem, smem],
         out_specs=vmem,
         scratch_shapes=[
             pltpu.VMEM((2, n, vecs, width), jnp.float32),
             pltpu.VMEM((n * row_tiles, 2 * vecs, TILE), jnp.bfloat16),
             pltpu.VMEM((groups, slots, TILE, TILE), jnp.float32),
-            pltpu.VMEM((groups * slots, TILE, 2 * TILE), jnp.bfloat16),
+            pltpu.VMEM((groups * slots, 2 * TILE, TILE), jnp.bfloat16),
             pltpu.VMEM((row_tiles, vecs, TILE), jnp.float32),
             pltpu.VMEM((vecs, width), jnp.float32),
             pltpu.VMEM((vecs, TILE), jnp.float32),
             pltpu.VMEM((PASSES, n - 1, 8, TILE), jnp.float32),
             pltpu.VMEM((PASSES, 8, TILE), jnp.float32),
-            dma((groups,)),
+            pltpu.SMEM((groups, slots), jnp.int32),
+            pltpu.SMEM((groups, slots), jnp.int32),
+            dma((groups,)), dma((3,)),
             dma((others, 2)), dma((2,)), dma((others,)), dma((others,)), dma,
             dma((others, 2)), dma((2,)), dma((others,)), dma((others,)),
             dma((2, others, 2)), dma((2, 2)), dma((2, others)), dma((2, others)), dma((2,)),
@@ -315,7 +317,7 @@
             dma((PASSES, n - 1)), dma((PASSES, n - 1)),
         ],
         compiler_params=pltpu.CompilerParams(
-            collective_id=0, has_side_effects=True, vmem_limit_bytes=48 * 2**20
+            collective_id=0, has_side_effects=True, vmem_limit_bytes=56 * 2**20
         ),
         cost_estimate=pl.CostEstimate(
             flops=PASSES * DEGREE * groups * slots * 8 * vecs * TILE * TILE,

time: 72 us -> 68.2 us (0.947)
  Pallas kernels: 67.6 us -> 65.2 us
  local copies, waits for them, and re-layouts: 2.92 us -> 1.57 us
    pallas_call x1, Pallas kernels: 67.6 us -> 65.2 us  [shards(): pl.pallas_call(body, out_shape=jax.ShapeDtypeStruct((vecs, width), jnp.fl...]
    unnamed x7 -> x1, local copies, waits for them, and re-layouts: 2.92 us -> 1.57 us
where the time goes in v1:
time: 68.2 us; the launch traced here: 68.1 us
  Pallas kernels  65.2 us (96%)
  local copies, waits for them, and re-layouts  1.57 us (2%)
  between operations  1.3 us (2%)
    pallas_call x1, Pallas kernels, shards(): pl.pallas_call(body, out_shape=jax.ShapeDtypeStruct((vecs, width), jnp.fl...  65.2 us
    unnamed x1, local copies, waits for them, and re-layouts  1.57 us

profile of v1, /device:TPU:0, one launch (start us, length us, event | category | flops | bytes accessed | tf_op | source)
XLA Modules:
  0.0 68.1 jit_solution(8839997104437687278)
XLA Ops:
  1.3 65.2 %shard_map.64 = f32[32,1024]{1,0:T(8,128)} custom-call(f32[32,1024]{1,0:T(8,128)} %vec_ref.1, f32[1,4,24,128,128]{4,3,2,1,0:T(8,128)} %ham_ref.1, s32[1,4,24]{2,1,0:T(4,128)} %rows_ref.1, s32[1,4,24]{2,1,0:T(4,128)} %cols_ref.1, f32[1]{0:T(128)S(6)} %copy.8.center_ref, f32[1]{0:T(128)S(6)} %copy.9.half_ref), custom_call_target="tpu_custom_call" | custom-call | flops 2415919104 | bytes 6291456 | tf_op jit(solution)/shard_map/pallas_call | solution.py:295
  66.5 1.6 %copy.10 = f32[32,1024]{1,0:T(8,128)} copy(f32[32,1024]{1,0:T(8,128)} %shard_map.64) | data formatting | bytes 262144

commit v2 on v1

v2 whole, which is shorter than its diff:
```python
import functools

import jax
import jax.numpy as jnp
from jax import lax
from jax.experimental import pallas as pl
from jax.experimental.pallas import tpu as pltpu
from jax.sharding import PartitionSpec as P

TILE = 128
PASSES = 2
DEGREE = 3
CORES = 2
STREAMS = 2


def kernel(
    n_blk, n_reader, total_cols,
    vec_ref, ham_ref, rows_ref, cols_ref, center_ref, half_ref,
    out_ref,
    blocks, sources, staged, weights, acc, before, scale, sums, partial_sum,
    rows_smem, cols_smem, ham_sem, in_sem,
    send_x, send_y, send_dx, send_dy, send_own, send_cx, send_cy, send_cdx, send_cdy,
    recv_x, recv_y, recv_dx, recv_dy, recv_own, recv_cx, recv_cy, recv_cdx, recv_cdy,
    send_sum, recv_sum,
):
    vecs = vec_ref.shape[0] // STREAMS
    row_tiles = vec_ref.shape[1] // TILE
    slots = rows_ref.shape[2]
    group_tiles = n_reader * row_tiles
    peers = n_blk * n_reader - 1
    half = vec_ref.shape[1] // 2
    halves = (pl.ds(0, half), pl.ds(half, half))

    blk = lax.axis_index("blk")
    x = lax.axis_index("reader")
    core = lax.rem(blk, CORES)
    side = blk - core
    blk_c = side + (1 - core)
    blk_y = lax.rem(blk + CORES, n_blk)
    blk_yc = lax.rem(blk_c + CORES, n_blk)
    me = blk * n_reader + x

    def peer(step):
        other = lax.rem(me + step, n_blk * n_reader)
        return {"blk": other // n_reader, "reader": lax.rem(other, n_reader)}

    def block_of(b, step=0):
        return b * n_reader + lax.rem(x + n_reader - step, n_reader)

    barrier = pltpu.get_barrier_semaphore()
    for step in range(1, peers + 1):
        pl.semaphore_signal(
            barrier, inc=1, device_id=peer(step), device_id_type=pl.DeviceIdType.MESH
        )

    def ham_copy(group):
        return pltpu.make_async_copy(
            ham_ref.at[0, group], staged.at[group], ham_sem.at[group]
        )

    loads = [
        *(pltpu.make_async_copy(vec_ref.at[pl.ds(st * vecs, vecs)], blocks.at[0, st, me],
                                in_sem.at[2 + st]) for st in range(STREAMS)),
        pltpu.make_async_copy(rows_ref.at[0], rows_smem, in_sem.at[0]),
        pltpu.make_async_copy(cols_ref.at[0], cols_smem, in_sem.at[1]),
    ]
    for copy in loads:
        copy.start()
    for group in (blk, blk_c, blk_y, blk_yc):
        ham_copy(group).start()
    scale[...] = jnp.ones_like(scale)
    before[...] = jnp.zeros_like(before)
    for copy in loads:
        copy.wait()
    pl.semaphore_wait(barrier, peers)

    def split_tiles(group):
        ham_copy(group).wait()

        def one(slot, carry):
            tile = staged[group, slot].T
            high = tile.astype(jnp.bfloat16)
            low = (tile - high.astype(jnp.float32)).astype(jnp.bfloat16)
            weights[group * slots + slot] = jnp.concatenate([high, low], axis=0)
            return carry

        lax.fori_loop(0, slots, one, 0)

    def split_block(st, par, index):
        for t in range(row_tiles):
            value = blocks[par, st, index, :, t * TILE : (t + 1) * TILE] * scale[st]
            high = value.astype(jnp.bfloat16).astype(jnp.float32)
            both = jnp.concatenate([high, value - high], axis=0)
            sources[st, index * row_tiles + t] = both.astype(jnp.bfloat16)

    def multiply(st, group):
        totals = [acc[st, t] for t in range(row_tiles)]
        for slot in range(slots):
            col = cols_smem[group, slot]
            row = rows_smem[group, slot]
            source = sources[st, group * group_tiles + col]
            product = jnp.dot(
                jnp.concatenate([source, source], axis=1),
                weights[group * slots + slot],
                preferred_element_type=jnp.float32,
            )
            product = product[:vecs] + product[vecs:]
            for t in range(row_tiles):
                totals[t] = totals[t] + jnp.where(row == t, product, 0.0)
        for t in range(row_tiles):
            acc[st, t] = totals[t]

    to_core = {"blk": blk_c}
    to_y = {"blk": blk_y}

    def to_x(step):
        return {"reader": lax.rem(x + step, n_reader)}

    steps = range(1, n_reader)
    x_block = [block_of(blk, s) for s in steps]
    y_block = block_of(blk_y)
    d_block = [block_of(blk_y, s) for s in steps]

    def copies(st, k):
        par = lax.rem(k, 2)

        def remote(index, part, send, recv, target):
            where = blocks.at[par, st, index]
            if part is not None:
                where = blocks.at[par, st, index, :, halves[part]]
            return pltpu.make_async_remote_copy(
                src_ref=where, dst_ref=where, send_sem=send, recv_sem=recv,
                device_id=target, device_id_type=pl.DeviceIdType.MESH,
            )

        return dict(
            x=[[remote(me, h, send_x.at[st, s - 1, h], recv_x.at[st, par, s - 1, h], to_x(s))
                for h in range(2)] for s in steps],
            y=[remote(me, h, send_y.at[st, h], recv_y.at[st, par, h], to_y) for h in range(2)],
            own=remote(me, None, send_own.at[st], recv_own.at[st, par], to_core),
            dy=[remote(x_block[s - 1], 0, send_dy.at[st, s - 1], recv_dy.at[st, par, s - 1],
                       to_y) for s in steps],
            dx=[remote(y_block, 1, send_dx.at[st, s - 1], recv_dx.at[st, par, s - 1], to_x(s))
                for s in steps],
            cx=[[remote(x_block[s - 1], h, send_cx.at[st, s - 1, h],
                        recv_cx.at[st, par, s - 1, h], to_core) for h in range(2)]
                for s in steps],
            cy=[remote(y_block, h, send_cy.at[st, h], recv_cy.at[st, par, h], to_core)
                for h in range(2)],
            cdy=[remote(d_block[s - 1], 0, send_cdy.at[st, s - 1], recv_cdy.at[st, par, s - 1],
                        to_core) for s in steps],
            cdx=[remote(d_block[s - 1], 1, send_cdx.at[st, s - 1], recv_cdx.at[st, par, s - 1],
                        to_core) for s in steps],
        )

    def sum_copy(st, turn, step):
        at = turn * STREAMS + st
        return pltpu.make_async_remote_copy(
            src_ref=partial_sum.at[at], dst_ref=sums.at[at, step - 1],
            send_sem=send_sum.at[at, step - 1], recv_sem=recv_sum.at[at, step - 1],
            device_id=peer(step), device_id_type=pl.DeviceIdType.MESH,
        )

    diagonal = (
        lax.broadcasted_iota(jnp.int32, (vecs, TILE), 0)
        == lax.broadcasted_iota(jnp.int32, (vecs, TILE), 1)
    )

    def share_sums(st, turn, squares):
        own = jnp.sum(squares, axis=1, keepdims=True)
        line = jnp.sum(jnp.where(diagonal, own, 0.0), axis=0, keepdims=True)
        partial_sum[turn * STREAMS + st] = jnp.broadcast_to(line, partial_sum.shape[1:])
        for step in range(1, peers + 1):
            sum_copy(st, turn, step).start()

    def norms(st, turn):
        for step in range(1, peers + 1):
            sum_copy(st, turn, step).wait()
        total = partial_sum[turn * STREAMS + st]
        for step in range(1, peers + 1):
            total = total + sums[turn * STREAMS + st, step - 1]
        spread = jnp.broadcast_to(total[:1], (vecs, TILE))
        squares = jnp.sum(jnp.where(diagonal, spread, 0.0), axis=1, keepdims=True)
        root = jnp.sqrt(squares / total_cols + 1e-06)
        return jnp.broadcast_to(1.0 / root, (vecs, TILE))

    def send(st, k):
        c = copies(st, k)
        for s in steps:
            c["x"][s - 1][0].start()
        c["y"][1].start()
        c["own"].start()
        for s in steps:
            c["x"][s - 1][1].start()
        c["y"][0].start()

    def pass_on(st, k):
        par = lax.rem(k, 2)
        c = copies(st, k)
        for s in steps:
            c["x"][s - 1][0].wait_recv()
            c["dy"][s - 1].start()
            c["cx"][s - 1][0].start()
        c["y"][1].wait_recv()
        for s in steps:
            c["dx"][s - 1].start()
        c["cy"][1].start()
        for s in steps:
            c["x"][s - 1][1].wait_recv()
            c["cx"][s - 1][1].start()
        c["y"][0].wait_recv()
        c["cy"][0].start()

        @pl.when(k == DEGREE)
        def _():
            scale[st] = norms(st, 0)

        @pl.when(k == DEGREE + 1)
        def _():
            scale[st] = jnp.ones_like(scale[st])

        split_block(st, par, me)
        for s in steps:
            split_block(st, par, x_block[s - 1])
        split_block(st, par, y_block)

    def near(st, k):
        par = lax.rem(k, 2)
        c = copies(st, k)
        acc[st] = jnp.zeros_like(acc[st])
        multiply(st, blk)
        c["own"].wait_recv()
        split_block(st, par, block_of(blk_c))
        for s in steps:
            for h in range(2):
                c["cx"][s - 1][h].wait_recv()
            split_block(st, par, block_of(blk_c, s))
        multiply(st, blk_c)

    def corner(st, k):
        par = lax.rem(k, 2)
        c = copies(st, k)
        for s in steps:
            c["dy"][s - 1].wait_recv()
            c["cdy"][s - 1].start()
            c["dx"][s - 1].wait_recv()
            c["cdx"][s - 1].start()
            split_block(st, par, d_block[s - 1])

    def far(st, k):
        par = lax.rem(k, 2)
        c = copies(st, k)
        multiply(st, blk_y)
        for h in range(2):
            c["cy"][h].wait_recv()
        split_block(st, par, block_of(blk_yc))
        for s in steps:
            c["cdy"][s - 1].wait_recv()
            c["cdx"][s - 1].wait_recv()
            split_block(st, par, block_of(blk_yc, s))
        multiply(st, blk_yc)

        first = lax.rem(k, DEGREE) == 0
        center = center_ref[0]
        gain = jnp.where(first, 1.0, 2.0) / half_ref[0]
        squares = jnp.zeros((vecs, TILE), jnp.float32)
        for t in range(row_tiles):
            lanes = slice(t * TILE, (t + 1) * TILE)
            field = blocks[par, st, me, :, lanes] * scale[st]
            new = (acc[st, t] - center * field) * gain
            new = new - jnp.where(first, 0.0, before[st, :, lanes])
            before[st, :, lanes] = field
            blocks[1 - par, st, me, :, lanes] = new
            squares = squares + new * new

        @pl.when(lax.rem(k, DEGREE) == DEGREE - 1)
        def _():
            share_sums(st, k // DEGREE, squares)

        c["own"].wait_send()
        for h in range(2):
            c["y"][h].wait_send()
            c["cy"][h].wait_send()
        for s in steps:
            for h in range(2):
                c["x"][s - 1][h].wait_send()
                c["cx"][s - 1][h].wait_send()
            for name in ("dx", "dy", "cdx", "cdy"):
                c[name][s - 1].wait_send()

        @pl.when(k + 1 < total_steps)
        def _():
            send(st, k + 1)

    total_steps = PASSES * DEGREE
    send(0, 0)
    send(1, 0)
    split_tiles(blk)
    split_tiles(blk_c)
    pass_on(0, 0)
    split_tiles(blk_y)
    split_tiles(blk_yc)

    def apply(k, carry):
        near(0, k)
        pass_on(1, k)
        corner(0, k)
        far(0, k)
        near(1, k)
        corner(1, k)

        @pl.when(k + 1 < total_steps)
        def _():
            pass_on(0, k + 1)

        far(1, k)
        return carry

    lax.fori_loop(0, total_steps, apply, 0)
    for st in range(STREAMS):
        last = norms(st, PASSES - 1)
        for t in range(row_tiles):
            lanes = slice(t * TILE, (t + 1) * TILE)
            out_ref[st * vecs : (st + 1) * vecs, lanes] = (
                blocks[total_steps % 2, st, me, :, lanes] * last
            )


def shards(n_blk, n_reader, vectors, ham_tiles, tile_rows, tile_cols, center, halfwidth):
    vecs, width = vectors.shape
    row_tiles = width // TILE
    n = n_blk * n_reader
    groups, slots = tile_rows.shape[1:]
    others = n_reader - 1
    q = STREAMS
    part = vecs // STREAMS
    dma = pltpu.SemaphoreType.DMA
    smem = pl.BlockSpec(memory_space=pltpu.SMEM)
    hbm = pl.BlockSpec(memory_space=pl.ANY)
    vmem = pl.BlockSpec(memory_space=pltpu.VMEM)
    body = functools.partial(kernel, n_blk, n_reader, n * width)
    return pl.pallas_call(
        body,
        out_shape=jax.ShapeDtypeStruct((vecs, width), jnp.float32),
        in_specs=[hbm, hbm, hbm, hbm, smem, smem],
        out_specs=vmem,
        scratch_shapes=[
            pltpu.VMEM((2, STREAMS, n, part, width), jnp.float32),
            pltpu.VMEM((STREAMS, n * row_tiles, 2 * part, TILE), jnp.bfloat16),
            pltpu.VMEM((groups, slots, TILE, TILE), jnp.float32),
            pltpu.VMEM((groups * slots, 2 * TILE, TILE), jnp.bfloat16),
            pltpu.VMEM((STREAMS, row_tiles, part, TILE), jnp.float32),
            pltpu.VMEM((STREAMS, part, width), jnp.float32),
            pltpu.VMEM((STREAMS, part, TILE), jnp.float32),
            pltpu.VMEM((PASSES * STREAMS, n - 1, 8, TILE), jnp.float32),
            pltpu.VMEM((PASSES * STREAMS, 8, TILE), jnp.float32),
            pltpu.SMEM((groups, slots), jnp.int32),
            pltpu.SMEM((groups, slots), jnp.int32),
            dma((groups,)), dma((4,)),
            dma((q, others, 2)), dma((q, 2)), dma((q, others)), dma((q, others)), dma((q,)),
            dma((q, others, 2)), dma((q, 2)), dma((q, others)), dma((q, others)),
            dma((q, 2, others, 2)), dma((q, 2, 2)), dma((q, 2, others)), dma((q, 2, others)),
            dma((q, 2)),
            dma((q, 2, others, 2)), dma((q, 2, 2)), dma((q, 2, others)), dma((q, 2, others)),
            dma((PASSES * q, n - 1)), dma((PASSES * q, n - 1)),
        ],
        compiler_params=pltpu.CompilerParams(
            collective_id=0, has_side_effects=True, vmem_limit_bytes=56 * 2**20
        ),
        cost_estimate=pl.CostEstimate(
            flops=PASSES * DEGREE * groups * slots * 8 * vecs * TILE * TILE,
            bytes_accessed=groups * slots * TILE * TILE * 4,
            transcendentals=0,
        ),
    )(vectors, ham_tiles, tile_rows, tile_cols, center, halfwidth)


def solution(mesh):
    n_blk, n_reader = mesh.shape["blk"], mesh.shape["reader"]
    return jax.shard_map(
        functools.partial(shards, n_blk, n_reader),
        mesh=mesh,
        in_specs=(
            P("bulk", ("blk", "reader")),
            P(("blk", "reader"), None, None, None, None),
            P(("blk", "reader"), None, None),
            P(("blk", "reader"), None, None),
            P(),
            P(),
        ),
        out_specs=P("bulk", ("blk", "reader")),
        check_vma=False,
    )
```

time: 68.2 us -> 74 us (1.085)
  Pallas kernels: 65.2 us -> 70.9 us
    pallas_call x1, Pallas kernels: 65.2 us -> 70.9 us  [shards(): pl.pallas_call(body, out_shape=jax.ShapeDtypeStruct((vecs, width), jnp.fl...]
where the time goes in v2:
time: 74 us; the launch traced here: 73.8 us
  Pallas kernels  70.9 us (96%)
  local copies, waits for them, and re-layouts  1.57 us (2%)
  between operations  1.3 us (2%)
    pallas_call x1, Pallas kernels, shards(): pl.pallas_call(body, out_shape=jax.ShapeDtypeStruct((vecs, width), jnp.fl...  70.9 us
    unnamed x1, local copies, waits for them, and re-layouts  1.57 us

profile of v2, /device:TPU:0, one launch (start us, length us, event | category | flops | bytes accessed | tf_op | source)
XLA Modules:
  0.0 73.8 jit_solution(17926629585975249324)
XLA Ops:
  1.3 70.9 %shard_map.64 = f32[32,1024]{1,0:T(8,128)} custom-call(f32[32,1024]{1,0:T(8,128)} %vec_ref.1, f32[1,4,24,128,128]{4,3,2,1,0:T(8,128)} %ham_ref.1, s32[1,4,24]{2,1,0:T(4,128)} %rows_ref.1, s32[1,4,24]{2,1,0:T(4,128)} %cols_ref.1, f32[1]{0:T(128)S(6)} %copy.8.center_ref, f32[1]{0:T(128)S(6)} %copy.9.half_ref), custom_call_target="tpu_custom_call" | custom-call | flops 2415919104 | bytes 6291456 | tf_op jit(solution)/shard_map/pallas_call | solution.py:343
  72.2 1.6 %copy.10 = f32[32,1024]{1,0:T(8,128)} copy(f32[32,1024]{1,0:T(8,128)} %shard_map.64) | data formatting | bytes 262144

commit v3 on v1

--- a/solution.py
+++ b/solution.py
@@ -80,7 +80,7 @@
             tile = staged[group, slot].T
             high = tile.astype(jnp.bfloat16)
             low = (tile - high.astype(jnp.float32)).astype(jnp.bfloat16)
-            weights[group * slots + slot] = jnp.concatenate([high, low], axis=0)
+            weights[group * slots + slot] = jnp.concatenate([high, low], axis=1)
             return carry
 
         lax.fori_loop(0, slots, one, 0)
@@ -99,11 +99,11 @@
             row = rows_smem[group, slot]
             source = sources[group * group_tiles + col]
             product = jnp.dot(
-                jnp.concatenate([source, source], axis=1),
+                source,
                 weights[group * slots + slot],
                 preferred_element_type=jnp.float32,
             )
-            product = product[:vecs] + product[vecs:]
+            product = product[:vecs, :TILE] + (product[vecs:, :TILE] + product[:vecs, TILE:])
             for t in range(row_tiles):
                 totals[t] = totals[t] + jnp.where(row == t, product, 0.0)
         for t in range(row_tiles):
@@ -301,7 +301,7 @@
             pltpu.VMEM((2, n, vecs, width), jnp.float32),
             pltpu.VMEM((n * row_tiles, 2 * vecs, TILE), jnp.bfloat16),
             pltpu.VMEM((groups, slots, TILE, TILE), jnp.float32),
-            pltpu.VMEM((groups * slots, 2 * TILE, TILE), jnp.bfloat16),
+            pltpu.VMEM((groups * slots, TILE, 2 * TILE), jnp.bfloat16),
             pltpu.VMEM((row_tiles, vecs, TILE), jnp.float32),
             pltpu.VMEM((vecs, width), jnp.float32),
             pltpu.VMEM((vecs, TILE), jnp.float32),

time: 68.2 us -> 68.1 us (level)
  no operation moved by 1% of the time
where the time goes in v3:
time: 68.1 us; the launch traced here: 67.9 us
  Pallas kernels  65 us (95%)
  local copies, waits for them, and re-layouts  1.57 us (2%)
  between operations  1.3 us (2%)
    pallas_call x1, Pallas kernels, shards(): pl.pallas_call(body, out_shape=jax.ShapeDtypeStruct((vecs, width), jnp.fl...  65 us
    unnamed x1, local copies, waits for them, and re-layouts  1.57 us

profile of v3, /device:TPU:0, one launch (start us, length us, event | category | flops | bytes accessed | tf_op | source)
XLA Modules:
  0.0 67.9 jit_solution(3530948003014519059)
XLA Ops:
  1.3 65.0 %shard_map.64 = f32[32,1024]{1,0:T(8,128)} custom-call(f32[32,1024]{1,0:T(8,128)} %vec_ref.1, f32[1,4,24,128,128]{4,3,2,1,0:T(8,128)} %ham_ref.1, s32[1,4,24]{2,1,0:T(4,128)} %rows_ref.1, s32[1,4,24]{2,1,0:T(4,128)} %cols_ref.1, f32[1]{0:T(128)S(6)} %copy.8.center_ref, f32[1]{0:T(128)S(6)} %copy.9.half_ref), custom_call_target="tpu_custom_call" | custom-call | flops 2415919104 | bytes 6291456 | tf_op jit(solution)/shard_map/pallas_call | solution.py:295
  66.3 1.6 %copy.10 = f32[32,1024]{1,0:T(8,128)} copy(f32[32,1024]{1,0:T(8,128)} %shard_map.64) | data formatting | bytes 262144

commit v4 on v1

--- a/solution.py
+++ b/solution.py
@@ -167,10 +167,9 @@
               for s in steps]
         dx = [remote(par, y_block, 1, send_dx.at[s - 1], recv_dx.at[par, s - 1], to_x(s))
               for s in steps]
-        cx = [[remote(par, x_block[s - 1], h, send_cx.at[s - 1, h],
-                      recv_cx.at[par, s - 1, h], to_core) for h in range(2)] for s in steps]
-        cy = [remote(par, y_block, h, send_cy.at[h], recv_cy.at[par, h], to_core)
-              for h in range(2)]
+        cx = [remote(par, x_block[s - 1], None, send_cx.at[s - 1, 0],
+                     recv_cx.at[par, s - 1, 0], to_core) for s in steps]
+        cy = remote(par, y_block, None, send_cy.at[0], recv_cy.at[par, 0], to_core)
         cdy = [remote(par, d_block[s - 1], 0, send_cdy.at[s - 1], recv_cdy.at[par, s - 1],
                       to_core) for s in steps]
         cdx = [remote(par, d_block[s - 1], 1, send_cdx.at[s - 1], recv_cdx.at[par, s - 1],
@@ -203,24 +202,21 @@
         for s in steps:
             x_own[s - 1][0].wait_recv()
             dy[s - 1].start()
-            cx[s - 1][0].start()
         y_own[1].wait_recv()
         for s in steps:
             dx[s - 1].start()
-        cy[1].start()
         for s in steps:
             x_own[s - 1][1].wait_recv()
-            cx[s - 1][1].start()
+            cx[s - 1].start()
             split_block(par, x_block[s - 1])
         y_own[0].wait_recv()
-        cy[0].start()
+        cy.start()
         split_block(par, y_block)
         c_own.wait_recv()
         split_block(par, block_of(blk_c))
         multiply(blk)
         for s in steps:
-            cx[s - 1][0].wait_recv()
-            cx[s - 1][1].wait_recv()
+            cx[s - 1].wait_recv()
             split_block(par, block_of(blk_c, s))
         multiply(blk_c)
 
@@ -236,8 +232,7 @@
             cdx[s - 1].start()
             split_block(par, d_block[s - 1])
         multiply(blk_y)
-        cy[1].wait_recv()
-        cy[0].wait_recv()
+        cy.wait_recv()
         split_block(par, block_of(blk_yc))
         for s in steps:
             cdy[s - 1].wait_recv()
@@ -265,12 +260,11 @@
         c_own.wait_send()
         for h in range(2):
             y_own[h].wait_send()
-            cy[h].wait_send()
+        cy.wait_send()
         for s in steps:
             for h in range(2):
                 x_own[s - 1][h].wait_send()
-                cx[s - 1][h].wait_send()
-            for copy in (dx, dy, cdx, cdy):
+            for copy in (dx, dy, cx, cdx, cdy):
                 copy[s - 1].wait_send()
         return carry
 

time: 68.2 us -> 68.1 us (level)
  no operation moved by 1% of the time
where the time goes in v4:
time: 68.1 us; the launch traced here: 68 us
  Pallas kernels  65.1 us (96%)
  local copies, waits for them, and re-layouts  1.57 us (2%)
  between operations  1.3 us (2%)
    pallas_call x1, Pallas kernels, shards(): pl.pallas_call(body, out_shape=jax.ShapeDtypeStruct((vecs, width), jnp.fl...  65.1 us
    unnamed x1, local copies, waits for them, and re-layouts  1.57 us

profile of v4, /device:TPU:0, one launch (start us, length us, event | category | flops | bytes accessed | tf_op | source)
XLA Modules:
  0.0 68.0 jit_solution(10267460583663139898)
XLA Ops:
  1.3 65.1 %shard_map.64 = f32[32,1024]{1,0:T(8,128)} custom-call(f32[32,1024]{1,0:T(8,128)} %vec_ref.1, f32[1,4,24,128,128]{4,3,2,1,0:T(8,128)} %ham_ref.1, s32[1,4,24]{2,1,0:T(4,128)} %rows_ref.1, s32[1,4,24]{2,1,0:T(4,128)} %cols_ref.1, f32[1]{0:T(128)S(6)} %copy.8.center_ref, f32[1]{0:T(128)S(6)} %copy.9.half_ref), custom_call_target="tpu_custom_call" | custom-call | flops 2415919104 | bytes 6291456 | tf_op jit(solution)/shard_map/pallas_call | solution.py:289
  66.4 1.6 %copy.10 = f32[32,1024]{1,0:T(8,128)} copy(f32[32,1024]{1,0:T(8,128)} %shard_map.64) | data formatting | bytes 262144
